TPU v7x, 32 devices: a whole 2x2x4 slice. The times are simulated.
32 devices in a mesh: groups: 2 (over y), dp: 4 (over z), chan: 2 (over x), sub: 2 (over core).
Axes of the slice: x: 2, y: 2, z: 4, core: 2. Of those that a mesh axis runs over, the one named last changes fastest.
Arguments:
- features: bfloat16 [192, 128, 1536], P(('groups', 'dp', 'sub'), None, 'chan'), parts along dimension 0, may hold values from -6 to 6
- cotangent: bfloat16 [192, 128, 1536], P(('groups', 'dp', 'sub'), None, 'chan'), parts along dimension 0, may hold values from -0.076171875 to 0.076171875
- snake_alpha: float32 [1536], P('chan'), may hold values from 0.5 to 4
- conv_weight: bfloat16 [1536, 3, 1536], P('dp', None, 'chan'), may hold values from -0.09375 to 0.09375
- lengths: int32 [192], P(('groups', 'dp', 'sub')), parts along dimension 0, may hold values from 1 to 128, as said below
- kept_rows: int32 [16], P(('groups', 'dp', 'sub')), parts along dimension 0, may hold values from 1 to 6, as said below
- sent_rows: int32 [16], P(('groups', 'dp', 'sub')), parts along dimension 0, may hold values from 0 to 6, as said below
Outputs:
- balanced_out: bfloat16 [112, 128, 1536], P(('groups', 'dp', 'sub'), None, 'chan'), parts along dimension 0
- weight_grad: float32 [3072, 3, 1536], P(('groups', 'dp'), None, 'chan'), parts along dimension 0
There are 2 independent parts, one for each index of `groups`. A program takes and returns all parts, laid end to end along the dimension named above; an argument that names none is the same for every part. Nothing has to cross between parts.
Inputs may be any that keep to these rules, and one draw needn't show every extreme that they name: `kept_rows`: each device keeps at least one row; one device keeps 6. kept_rows[h] + sent_rows[p] <= 7 for every device h and its previous device p; some device hands on 6 rows and some none. The first slot of every device has length 128; lengths of empty slots are not read.
All inputs are finite; a program needn't handle non-finite values.
Results may differ from a plain program's by a relative error of at most 0.01.
Values may be sent and summed in bfloat16 or wider, within the bound.
A program may use at most 128 MiB of HBM per device.

v0:
```python
import jax
import jax.numpy as jnp
from jax import lax
from jax.sharding import PartitionSpec as P

KERNEL_TAPS = 3
DILATION_STEP = 3


def from_behind(value, axis, by):
    devices = lax.axis_size(axis)
    return lax.ppermute(value, axis, [(i, (i + by) % devices) for i in range(devices)])


def snake_rows(rows, snake_alpha, time_mask):
    values = rows.astype(jnp.float32)
    shaped = values + jnp.sin(snake_alpha * values) ** 2 / snake_alpha
    return (shaped * time_mask[:, :, None]).astype(jnp.bfloat16)


def on_device(features, cotangent, snake_alpha, conv_weight, lengths, kept_rows, sent_rows):
    slots_in = features.shape[0]
    keep_count = slots_in // 2
    capacity = keep_count + 1
    step_total = features.shape[1]
    chan_width = features.shape[2]
    own_keep = kept_rows[0]
    own_sent = sent_rows[0]
    move_slots = jnp.arange(keep_count)
    keep_slots = jnp.arange(keep_count)
    moved_feat = lax.dynamic_slice_in_dim(features, own_keep, keep_count, 0)
    moved_cot = lax.dynamic_slice_in_dim(cotangent, own_keep, keep_count, 0)
    moved_len = jnp.where(
        move_slots < own_sent, lax.dynamic_slice_in_dim(lengths, own_keep, keep_count, 0), 0
    ).astype(jnp.bfloat16)
    arrived_feat, arrived_cot, arrived_len = from_behind(
        (moved_feat, moved_cot, moved_len), "dp", 1
    )

    def place_rows(own_part, arrived):
        blank_rows = jnp.zeros((keep_count,) + own_part.shape[1:], own_part.dtype)
        buffer = jnp.concatenate([own_part, blank_rows], axis=0)
        buffer = lax.dynamic_update_slice_in_dim(buffer, arrived, own_keep, 0)
        return buffer[:capacity]

    own_len = jnp.where(keep_slots < own_keep, lengths[:keep_count], 0)
    rows_bal = place_rows(features[:keep_count], arrived_feat)
    cot_bal = place_rows(cotangent[:keep_count], arrived_cot)
    len_bal = place_rows(own_len, arrived_len.astype(jnp.int32))
    time_mask = (jnp.arange(step_total)[None, :] < len_bal[:, None]).astype(jnp.float32)
    local_act = snake_rows(rows_bal, snake_alpha, time_mask)
    complete_output = lax.all_gather(local_act, "chan", axis=2, tiled=True)
    padded_width = complete_output.shape[2]
    padded_input = jnp.pad(complete_output, ((0, 0), (DILATION_STEP, DILATION_STEP), (0, 0)))
    flattened_rows = capacity * step_total
    shifted_tap_rows = [
        padded_input[
            :, tap_number * DILATION_STEP : tap_number * DILATION_STEP + step_total, :
        ].reshape(flattened_rows, padded_width)
        for tap_number in range(KERNEL_TAPS)
    ]
    running = jnp.zeros((flattened_rows, chan_width), jnp.float32)
    panel_rows = lax.all_gather(conv_weight, "dp", axis=0, tiled=True)
    for tap_number in range(KERNEL_TAPS):
        columns = shifted_tap_rows[tap_number]
        running = running + jnp.dot(
            columns, panel_rows[:, tap_number, :], preferred_element_type=jnp.float32
        )
    result = (
        rows_bal.astype(jnp.float32) + running.reshape(capacity, step_total, chan_width)
    ) * time_mask[:, :, None]
    balanced_out = result.astype(jnp.bfloat16)
    cot_mask = jnp.where(time_mask[:, :, None] > 0.0, cot_bal, jnp.zeros_like(cot_bal)).reshape(
        flattened_rows, chan_width
    )
    products = []
    for tap_number in range(KERNEL_TAPS):
        columns = shifted_tap_rows[tap_number]
        products.append(
            lax.dot_general(
                columns, cot_mask, (((0,), (0,)), ((), ())), preferred_element_type=jnp.float32
            )
        )
    shard_sum = lax.psum_scatter(
        jnp.stack(products, axis=1).astype(jnp.bfloat16), "dp", scatter_dimension=0, tiled=True
    )
    weight_grad = lax.psum(shard_sum, "sub").astype(jnp.float32)
    return (balanced_out, weight_grad)


def solution(mesh):
    placed = (
        P(("groups", "dp", "sub"), None, "chan"),
        P(("groups", "dp", "sub"), None, "chan"),
        P("chan"),
        P("dp", None, "chan"),
        P(("groups", "dp", "sub")),
        P(("groups", "dp", "sub")),
        P(("groups", "dp", "sub")),
    )
    return jax.shard_map(
        on_device,
        mesh=mesh,
        in_specs=placed,
        out_specs=(P(("groups", "dp", "sub"), None, "chan"), P(("groups", "dp"), None, "chan")),
        check_vma=False,
    )
```

profile of v0, /device:TPU:0, one launch (start us, length us, event | category | flops | bytes accessed | tf_op | source)
XLA Modules:
  0.0 383.4 jit_solution(10857712576062909988)
XLA Ops:
  7.2 0.0 all-gather.3.cloned.1.call-start
  7.9 0.0 copy-start.8
  7.9 3.0 copy.18
  10.9 0.0 copy-start
  10.9 1.2 constant_dynamic-slice_fusion.1
  12.1 3.0 collective-permute-start
  15.8 0.0 copy-done.8
  15.8 0.1 fusion.17
  15.9 1.6 collective-permute-start.1
  17.5 0.0 copy-done
  17.5 3.0 copy.24
  20.5 0.0 copy-done.9
  20.5 0.0 copy-start.7
  20.6 3.5 broadcast_select_fusion
  24.0 19.4 %collective-permute-done.1 = bf16[6]{0:T(256)(128)(2,1)S(1)} collective-permute-done((bf16[6]{0:T(256)(128)(2,1)S(1)}, bf16[6]{0:T(256)(128)(2,1)S(1)}, u32[]{:S(2)}, u32[]{:S(2)}) %collective-permute-start.1) | collective-permute-done | bytes 44 | tf_op jit(solution)/shard_map/ppermute | solution.py:12
  43.4 0.1 convert_dynamic-update-slice_fusion
  43.5 0.1 broadcast_compare_fusion
  43.6 0.0 collective-permute-done
  43.6 0.2 constant_dynamic-update-slice_fusion.1
  43.8 0.0 copy-start.1
  43.8 1.4 copy-done.1
  45.2 0.0 copy-done.7
  45.2 10.8 %fusion.7 = bf16[7,128,768]{1,2,0:T(8,128)(2,1)} fusion(f32[7,128]{1,0:T(8,128)S(1)} %get-tuple-element.9, f32[768]{0:T(1024)S(1)} %copy-done.7, bf16[12,128,768]{1,2,0:T(8,128)(2,1)S(1)} %constant_dynamic-update-slice_fusion.1), kind=kLoop, calls=%fused_computation.16 | loop fusion | flops 4816896 | bytes 2759168 | tf_op jit(solution)/shard_map/convert_element_type | solution.py:18
  55.9 0.0 all-gather.3.cloned.1.call-update
  56.0 0.0 all-gather.5.cloned.1.call-start
  56.0 0.7 all-gather.5.cloned.1.call-update
  56.7 0.0 reduce-scatter.2.cloned.1.call-start
  56.8 0.1 constant_dynamic-slice_fusion
  56.8 0.1 collective-permute-start.2
  56.9 28.9 %collective-permute-done.2 = bf16[6,128,768]{1,2,0:T(8,128)(2,1)S(1)} collective-permute-done((bf16[6,128,768]{1,2,0:T(8,128)(2,1)S(1)}, bf16[6,128,768]{1,2,0:T(8,128)(2,1)S(1)}, u32[]{:S(2)}, u32[]{:S(2)}) %collective-permute-start.2) | collective-permute-done | bytes 1179680 | tf_op jit(solution)/shard_map/ppermute | solution.py:12
  85.8 1.1 constant_dynamic-update-slice_fusion
  86.9 9.1 %all-gather.3.cloned.1.call-done = bf16[7,128,1536]{1,2,0:T(8,128)(2,1)} async-done(((bf16[7,128,768]{1,2,0:T(8,128)(2,1)}), bf16[7,128,1536]{1,2,0:T(8,128)(2,1)}) %all-gather.3.cloned.1.call-update) | async-done | bytes 2752528 | tf_op jit(solution)/shard_map/all_gather | solution.py:52
  96.0 0.0 copy-start.3
  96.0 0.0 copy-start.6
  96.0 5.0 %fusion = bf16[1536,1,768]{2,0,1:T(8,128)(2,1)S(1)} fusion(bf16[12,128,768]{1,2,0:T(8,128)(2,1)} %constant_dynamic-update-slice_fusion, pred[7,128]{1,0:T(8,128)(4,1)S(1)} %get-tuple-element.8, bf16[7,128,1536]{1,2,0:T(8,128)(2,1)} %all-gather.3.cloned.1.call-done), kind=kOutput, calls=%fused_computation.9 | convolution fusion | flops 2115796992 | bytes 6488960 | tf_op jit(solution)/shard_map/dot_general | solution.py:80
  101.0 0.0 copy-done.3
  101.0 0.0 copy-done.6
  101.0 2.9 fusion.2
  103.9 2.9 fusion.1
  106.8 3.5 pad_maximum_fusion
  110.3 0.0 reduce-scatter.2.cloned.1.call-update
  110.3 0.2 all-reduce.4.cloned.1.call-start
  110.5 3.3 pad_slice_fusion.1
  113.8 4.6 %copy.22 = bf16[7,128,1536]{2,1,0:T(8,128)(2,1)} copy(bf16[7,128,1536]{1,2,0:T(8,128)(2,1)} %get-tuple-element.7) | data formatting | bytes 5505024 | tf_op jit(solution)/shard_map/slice | solution.py:57
  118.4 4.7 %copy.20 = bf16[7,128,1536]{2,1,0:T(8,128)(2,1)} copy(bf16[7,128,1536]{1,2,0:T(8,128)(2,1)} %get-tuple-element.6) | data formatting | bytes 5505024 | tf_op jit(solution)/shard_map/slice | solution.py:57
  123.1 2.8 copy.21
  126.0 99.9 %all-gather.5.cloned.1.call-done = bf16[1536,3,768]{2,0,1:T(8,128)(2,1)} async-done(((bf16[384,3,768]{2,0,1:T(8,128)(2,1)}), bf16[1536,3,768]{2,0,1:T(8,128)(2,1)}) %all-gather.5.cloned.1.call-update) | async-done | bytes 7077904 | tf_op jit(solution)/shard_map/all_gather | solution.py:63
  225.8 0.0 copy-start.5
  225.8 6.5 %fusion.10 = f32[896,768]{1,0:T(8,128)} fusion(bf16[896,1536]{1,0:T(8,128)(2,1)} %bitcast.47, bf16[1536,3,768]{2,0,1:T(8,128)(2,1)} %all-gather.5.cloned.1.call-done), kind=kOutput, calls=%fused_computation.21 | convolution fusion | flops 2113929216 | bytes 7864320 | tf_op jit(solution)/shard_map/dot_general | solution.py:66
  232.3 117.5 %reduce-scatter.2.cloned.1.call-done = bf16[384,3,768]{2,0,1:T(8,128)(2,1)} async-done(((bf16[1536,3,768]{2,0,1:T(8,128)(2,1)}), bf16[384,3,768]{2,0,1:T(8,128)(2,1)}) %reduce-scatter.2.cloned.1.call-update) | async-done | bytes 1769488 | tf_op jit(solution)/shard_map/reduce_scatter | solution.py:84
  349.8 0.0 all-reduce.4.cloned.1.call-update
  349.9 0.0 copy-done.5
  349.9 0.0 copy-start.4
  349.9 0.0 copy-start.10
  349.9 4.1 %fusion.11 = f32[896,768]{1,0:T(8,128)S(1)} fusion(bf16[896,1536]{1,0:T(8,128)(2,1)S(1)} %bitcast.46, bf16[1536,3,768]{2,0,1:T(8,128)(2,1)} %all-gather.5.cloned.1.call-done), kind=kOutput, calls=%fused_computation.23 | convolution fusion | flops 2113929216 | bytes 7864320 | tf_op jit(solution)/shard_map/dot_general | solution.py:66
  354.0 0.0 copy-done.4
  354.0 0.0 copy-done.10
  354.0 5.5 %add_add_fusion = f32[896,768]{1,0:T(8,128)} fusion(f32[896,768]{1,0:T(8,128)S(1)} %copy-done.10, f32[896,768]{1,0:T(8,128)S(1)} %fusion.11, bf16[896,1536]{1,0:T(8,128)(2,1)S(1)} %bitcast.45, bf16[1536,3,768]{2,0,1:T(8,128)(2,1)} %all-gather.5.cloned.1.call-done), kind=kOutput, calls=%fused_computation.19 | convolution fusion | flops 2115305472 | bytes 13369344 | tf_op jit(solution)/shard_map/dot_general | solution.py:66
  359.5 3.6 copy.23
  363.1 0.0 copy-done.2
  363.1 3.2 fusion.9
  366.3 2.5 copy.29
  368.8 4.5 %all-reduce.4.cloned.1.call-done = bf16[384,3,768]{2,0,1:T(8,128)(2,1)} async-done(((bf16[384,3,768]{2,0,1:T(8,128)(2,1)}), bf16[384,3,768]{2,0,1:T(8,128)(2,1)}) %all-reduce.4.cloned.1.call-update) | async-done | bytes 1769488 | tf_op jit(solution)/shard_map/psum | solution.py:87
  373.3 3.6 convert_element_type.38
  (3 shorter events, 0.0 us)
Async XLA Ops:
  7.2 88.8 %all-gather.3.cloned.1.call-start = ((), (), s32[]{:S(2)}) async-start(), calls=%async_computation.1 | async-start | bytes 4128768 | tf_op jit(solution)/shard_map/all_gather | solution.py:52
  7.9 8.0 %copy-start.8 = (s32[12]{0:T(128)S(1)}, s32[12]{0:T(128)}, u32[]{:S(2)}) copy-start(s32[12]{0:T(128)} %param.11) | copy-start | bytes 148
  10.9 6.6 %copy-start = (bf16[12,128,768]{1,2,0:T(8,128)(2,1)}, bf16[12,128,768]{1,2,0:T(8,128)(2,1)S(1)}, u32[]{:S(2)}) copy-start(bf16[12,128,768]{1,2,0:T(8,128)(2,1)S(1)} %copy.18) | copy-start | bytes 7077892
  12.1 8.4 %copy-start.9 = (pred[12]{0:T(512)(128)(4,1)S(1)}, pred[12]{0:T(512)(128)(4,1)}, u32[]{:S(2)}) copy-start(pred[12]{0:T(512)(128)(4,1)} %constant.5.clone.1) | copy-start | bytes 40
  12.1 31.5 %collective-permute-start = (bf16[6,128,768]{1,2,0:T(8,128)(2,1)}, bf16[6,128,768]{1,2,0:T(8,128)(2,1)S(1)}, u32[]{:S(2)}, u32[]{:S(2)}) collective-permute-start(bf16[6,128,768]{1,2,0:T(8,128)(2,1)} %constant_dynamic-slice_fusion.1), channel_id=1, source_target_pairs={{0,4},{4,8},{8,12},{12,0},{1,5},{5,9},{9,13},{13,1},{2,6},{6,10},{... | collective-permute-start | bytes 3538952 | tf_op jit(solution)/shard_map/ppermute | solution.py:12
  15.9 27.5 %collective-permute-start.1 = (bf16[6]{0:T(256)(128)(2,1)S(1)}, bf16[6]{0:T(256)(128)(2,1)S(1)}, u32[]{:S(2)}, u32[]{:S(2)}) collective-permute-start(bf16[6]{0:T(256)(128)(2,1)S(1)} %get-tuple-element.12), channel_id=1, source_target_pairs={{0,4},{4,8},{8,12},{12,0},{1,5},{5,9},{9,13},{13,1},{2,6},{6,10},{... | collective-permute-start | bytes 44 | tf_op jit(solution)/shard_map/ppermute | solution.py:12
  20.5 24.6 %copy-start.7 = (f32[768]{0:T(1024)S(1)}, f32[768]{0:T(1024)}, u32[]{:S(2)}) copy-start(f32[768]{0:T(1024)} %param.9) | copy-start | bytes 9220
  43.8 1.4 copy-start.1
  56.0 169.9 %all-gather.5.cloned.1.call-start = ((), (), s32[]{:S(2)}) async-start(), calls=%async_computation.2 | async-start | bytes 8847360 | tf_op jit(solution)/shard_map/all_gather | solution.py:63
  56.7 293.1 %reduce-scatter.2.cloned.1.call-start = ((), (), s32[]{:S(2)}) async-start(), calls=%async_computation.3 | async-start | bytes 8847360 | tf_op jit(solution)/shard_map/reduce_scatter | solution.py:84
  56.8 28.9 %collective-permute-start.2 = (bf16[6,128,768]{1,2,0:T(8,128)(2,1)S(1)}, bf16[6,128,768]{1,2,0:T(8,128)(2,1)S(1)}, u32[]{:S(2)}, u32[]{:S(2)}) collective-permute-start(bf16[6,128,768]{1,2,0:T(8,128)(2,1)S(1)} %constant_dynamic-slice_fusion), channel_id=1, source_target_pairs={{0,4},{4,8},{8,12},{12,0},{1,5},{5,9},{9,13},{13,1},{2,6},{6,10},{... | collective-permute-start | bytes 3538952 | tf_op jit(solution)/shard_map/ppermute | solution.py:12
  96.0 5.0 %copy-start.3 = (bf16[7,128,1536]{1,2,0:T(8,128)(2,1)S(1)}, bf16[7,128,1536]{1,2,0:T(8,128)(2,1)}, u32[]{:S(2)}) copy-start(bf16[7,128,1536]{1,2,0:T(8,128)(2,1)} %all-gather.3.cloned.1.call-done) | copy-start | bytes 8257540
  96.0 5.0 %copy-start.6 = (bf16[12,128,768]{1,2,0:T(8,128)(2,1)S(1)}, bf16[12,128,768]{1,2,0:T(8,128)(2,1)}, u32[]{:S(2)}) copy-start(bf16[12,128,768]{1,2,0:T(8,128)(2,1)} %constant_dynamic-update-slice_fusion) | copy-start | bytes 7077892
  110.3 263.0 %all-reduce.4.cloned.1.call-start = ((), (), s32[]{:S(2)}) async-start(), calls=%async_computation.4 | async-start | bytes 3538944 | tf_op jit(solution)/shard_map/psum | solution.py:87
  225.8 124.0 %copy-start.5 = (bf16[7,128,1536]{2,1,0:T(8,128)(2,1)S(1)}, bf16[7,128,1536]{2,1,0:T(8,128)(2,1)}, u32[]{:S(2)}) copy-start(bf16[7,128,1536]{2,1,0:T(8,128)(2,1)} %copy.21) | copy-start | bytes 8257540
  349.9 4.1 %copy-start.4 = (bf16[7,128,1536]{2,1,0:T(8,128)(2,1)S(1)}, bf16[7,128,1536]{2,1,0:T(8,128)(2,1)}, u32[]{:S(2)}) copy-start(bf16[7,128,1536]{2,1,0:T(8,128)(2,1)} %copy.20) | copy-start | bytes 8257540
  349.9 4.1 %copy-start.10 = (f32[896,768]{1,0:T(8,128)S(1)}, f32[896,768]{1,0:T(8,128)}, u32[]{:S(2)}) copy-start(f32[896,768]{1,0:T(8,128)} %fusion.10) | copy-start | bytes 8257540
  359.5 3.6 copy-start.2
Sparse Core Ops, SparseCore 0:
  56.1 39.8 all-gather.2
  97.6 128.2 all-gather.4
  228.1 121.6 reduce-scatter.1
  352.0 21.2 all-reduce.3
where the time goes:
time: 384 us; the launch traced here: 383 us
  waiting for transfers between devices  280 us (73%)
  local copies, waits for them, and re-layouts  31.6 us (8%)
  matrix products  26.8 us (7%)
  other arithmetic  24.7 us (6%)
  between operations  15.3 us (4%)
  starting transfers between devices  5 us (1%)
    reduce_scatter x1, waiting for transfers between devices, on_device(): lax.psum_scatter(jnp.stack(products, axis=1).astype(jnp.bfloat16), 'dp',...  118 us
    all_gather x1, waiting for transfers between devices, on_device(): panel_rows = lax.all_gather(conv_weight, 'dp', axis=0, tiled=True)  99.9 us
    ppermute x3, waiting for transfers between devices, from_behind(): lax.ppermute(value, axis, [(i, (i + by) % devices) for i in range(devices)])  48.3 us
    dot_general x3, matrix products, on_device(): jnp.dot(columns, panel_rows[:, tap_number, :], preferred_element_type=jnp...  16.1 us
    slice x3, local copies, waits for them, and re-layouts, on_device(): padded_input[:, tap_number * DILATION_STEP:tap_number * DILATION_STEP + s...  12.6 us
    dot_general x3, matrix products, on_device(): lax.dot_general(columns, cot_mask, (((0,), (0,)), ((), ())), preferred_el...  10.8 us
    convert_element_type x1, other arithmetic, snake_rows(): return (shaped * time_mask[:, :, None]).astype(jnp.bfloat16)  10.8 us
    unnamed x25, local copies, waits for them, and re-layouts  10 us
  transfers between devices with their start and end apart: 7, of which 6 were waited for; matrix products, arithmetic and copies ran while one was open for 16% of the time, Pallas kernels for 0%

commit v1 on v0

--- a/solution.py
+++ b/solution.py
@@ -49,7 +49,20 @@
     len_bal = place_rows(own_len, arrived_len.astype(jnp.int32))
     time_mask = (jnp.arange(step_total)[None, :] < len_bal[:, None]).astype(jnp.float32)
     local_act = snake_rows(rows_bal, snake_alpha, time_mask)
-    complete_output = lax.all_gather(local_act, "chan", axis=2, tiled=True)
+    then, small, view_out = (lax.axis_size("chan"), lax.axis_index("chan"), local_act.shape[2])
+    r_now, big = (local_act, 1)
+    while big < then:
+        r_now = jnp.concatenate(
+            [
+                r_now,
+                lax.ppermute(
+                    r_now, axis_name="chan", perm=[(h, (h - big) % then) for h in range(then)]
+                ),
+            ],
+            axis=2,
+        )
+        big = 2 * big
+    complete_output = jnp.roll(r_now, small * view_out, axis=2)
     padded_width = complete_output.shape[2]
     padded_input = jnp.pad(complete_output, ((0, 0), (DILATION_STEP, DILATION_STEP), (0, 0)))
     flattened_rows = capacity * step_total

time: 384 us -> 355 us (0.924)
  waiting for transfers between devices: 280 us -> 224 us
  starting transfers between devices: 5 us -> 29.4 us
  other arithmetic: 24.7 us -> 29.5 us
    all_gather x1, waiting for transfers between devices: 99.9 us -> 2.74 us  [on_device(): panel_rows = lax.all_gather(conv_weight, 'dp', axis=0, tiled=True)]
    ppermute x3, waiting for transfers between devices: 48.3 us -> 85.9 us  [from_behind(): lax.ppermute(value, axis, [(i, (i + by) % devices) for i in range(devices)])]
    ppermute x3, starting transfers between devices: 4.66 us -> 27.3 us  [from_behind(): lax.ppermute(value, axis, [(i, (i + by) % devices) for i in range(devices)])]
    reduce_scatter x1, waiting for transfers between devices: 118 us -> 130 us  [on_device(): lax.psum_scatter(jnp.stack(products, axis=1).astype(jnp.bfloat16), 'dp',...]
    all_gather x1 -> x0, waiting for transfers between devices: 9.13 us -> none  [on_device(): complete_output = lax.all_gather(local_act, 'chan', axis=2, tiled=True)]
    concatenate x0 -> x1, other arithmetic: none -> 5.21 us  [on_device(): complete_output = jnp.roll(r_now, small * view_out, axis=2)]
    unnamed x25 -> x27, local copies, waits for them, and re-layouts: 10 us -> 10.1 us
  transfers between devices with their start and end apart: 7 -> 7, of which waited for: 6 -> 5; matrix products, arithmetic and copies ran while one was open for 16% -> 23% of each run, Pallas kernels for 0% -> 0%
where the time goes in v1:
time: 355 us; the launch traced here: 354 us
  waiting for transfers between devices  224 us (63%)
  local copies, waits for them, and re-layouts  30.9 us (9%)
  other arithmetic  29.5 us (8%)
  starting transfers between devices  29.4 us (8%)
  matrix products  24.8 us (7%)
  between operations  15.2 us (4%)
    reduce_scatter x1, waiting for transfers between devices, on_device(): lax.psum_scatter(jnp.stack(products, axis=1).astype(jnp.bfloat16), 'dp',...  130 us
    ppermute x3, waiting for transfers between devices, from_behind(): lax.ppermute(value, axis, [(i, (i + by) % devices) for i in range(devices)])  85.9 us
    ppermute x3, starting transfers between devices, from_behind(): lax.ppermute(value, axis, [(i, (i + by) % devices) for i in range(devices)])  27.3 us
    dot_general x3, matrix products, on_device(): jnp.dot(columns, panel_rows[:, tap_number, :], preferred_element_type=jnp...  16.1 us
    slice x3, local copies, waits for them, and re-layouts, on_device(): padded_input[:, tap_number * DILATION_STEP:tap_number * DILATION_STEP + s...  10.9 us
    convert_element_type x1, other arithmetic, snake_rows(): return (shaped * time_mask[:, :, None]).astype(jnp.bfloat16)  10.1 us
    unnamed x27, local copies, waits for them, and re-layouts  10.1 us
    dot_general x3, matrix products, on_device(): lax.dot_general(columns, cot_mask, (((0,), (0,)), ((), ())), preferred_el...  8.71 us
  transfers between devices with their start and end apart: 7, of which 5 were waited for; matrix products, arithmetic and copies ran while one was open for 23% of the time, Pallas kernels for 0%

profile of v1, /device:TPU:0, one launch (start us, length us, event | category | flops | bytes accessed | tf_op | source)
XLA Modules:
  0.0 354.4 jit_solution(1191575255116587250)
XLA Ops:
  7.2 0.0 all-gather.2.cloned.1.call-start
  7.2 0.7 all-gather.2.cloned.1.call-update
  7.9 0.0 reduce-scatter.2.cloned.1.call-start
  8.6 0.0 copy-start.9
  8.6 3.0 copy.18
  11.7 1.1 constant_dynamic-slice_fusion.1
  12.8 3.0 collective-permute-start
  16.4 0.0 copy-done.9
  16.4 0.1 fusion.20
  16.5 1.6 collective-permute-start.1
  18.1 4.5 %copy.24 = bf16[12,128,768]{1,2,0:T(8,128)(2,1)} copy(bf16[12,128,768]{2,1,0:T(8,128)(2,1)} %param.8) | data formatting | bytes 4718592 | tf_op args[1]
  22.6 0.0 copy-done.10
  22.6 0.0 copy-start.8
  22.6 3.8 %broadcast_select_fusion = (bf16[12,128,768]{1,2,0:T(8,128)(2,1)}, bf16[12,128,768]{1,2,0:T(8,128)(2,1)S(1)}) fusion(bf16[12,128,768]{1,2,0:T(8,128)(2,1)} %copy.24, pred[12]{0:T(512)(128)(4,1)S(1)} %copy-done.10, bf16[12,128,768]{1,2,0:T(8,128)(2,1)S(1)} %copy.18), kind=kLoop, calls=%fused_computation.33 | loop fusion | flops 2359296 | bytes 9437196 | tf_op jit(solution)/shard_map/concatenate | solution.py:42
  26.3 0.0 copy-start
  26.4 36.6 %collective-permute-done.1 = bf16[6]{0:T(256)(128)(2,1)S(1)} collective-permute-done((bf16[6]{0:T(256)(128)(2,1)S(1)}, bf16[6]{0:T(256)(128)(2,1)S(1)}, u32[]{:S(2)}, u32[]{:S(2)}) %collective-permute-start.1) | collective-permute-done | bytes 44 | tf_op jit(solution)/shard_map/ppermute | solution.py:12
  62.9 0.1 convert_dynamic-update-slice_fusion
  63.0 0.1 broadcast_compare_fusion
  63.1 0.0 collective-permute-done
  63.1 0.2 constant_dynamic-update-slice_fusion.1
  63.3 0.0 copy-start.1
  63.3 0.0 copy-done.8
  63.3 10.1 %fusion.7 = bf16[7,128,768]{1,2,0:T(8,128)(2,1)S(1)} fusion(f32[7,128]{1,0:T(8,128)S(1)} %get-tuple-element.9, f32[768]{0:T(1024)S(1)} %copy-done.8, bf16[12,128,768]{1,2,0:T(8,128)(2,1)S(1)} %constant_dynamic-update-slice_fusion.1), kind=kLoop, calls=%fused_computation.20 | loop fusion | flops 4816896 | bytes 2759168 | tf_op jit(solution)/shard_map/convert_element_type | solution.py:18
  73.4 0.0 copy-start.4
  73.4 1.8 collective-permute-start.2
  75.2 0.0 copy-done
  75.2 1.1 constant_dynamic-slice_fusion
  76.3 0.0 copy-done.1
  76.3 22.7 %collective-permute-start.3 = (bf16[6,128,768]{1,2,0:T(8,128)(2,1)}, bf16[6,128,768]{1,2,0:T(8,128)(2,1)S(1)}, u32[]{:S(2)}, u32[]{:S(2)}) collective-permute-start(bf16[6,128,768]{1,2,0:T(8,128)(2,1)} %constant_dynamic-slice_fusion), channel_id=1, source_target_pairs={{0,4},{4,8},{8,12},{12,0},{1,5},{5,9},{9,13},{13,1},{2,6},{6,10},{... | collective-permute-start | bytes 3538952 | tf_op jit(solution)/shard_map/ppermute | solution.py:12
  99.0 49.3 %collective-permute-done.3 = bf16[6,128,768]{1,2,0:T(8,128)(2,1)S(1)} collective-permute-done((bf16[6,128,768]{1,2,0:T(8,128)(2,1)}, bf16[6,128,768]{1,2,0:T(8,128)(2,1)S(1)}, u32[]{:S(2)}, u32[]{:S(2)}) %collective-permute-start.3) | collective-permute-done | bytes 1179680 | tf_op jit(solution)/shard_map/ppermute | solution.py:12
  148.4 1.2 constant_dynamic-update-slice_fusion
  149.5 0.0 copy-done.4
  149.5 0.0 copy-start.7
  149.5 0.0 collective-permute-done.2
  149.5 5.2 %fusion.12 = bf16[7,128,1536]{1,2,0:T(8,128)(2,1)S(1)} fusion(s32[]{:T(128)S(6)} %select_n.36, bf16[7,128,768]{1,2,0:T(8,128)(2,1)} %copy-done.4, bf16[7,128,768]{1,2,0:T(8,128)(2,1)} %collective-permute-done.2), kind=kLoop, calls=%fused_computation.25 | loop fusion | flops 11010048 | bytes 5505028 | tf_op jit(solution)/shard_map/jit(_roll_dynamic)/concatenate | solution.py:65
  154.7 0.0 copy-done.7
  154.8 2.9 fusion
  157.7 2.9 fusion.2
  160.6 2.9 fusion.1
  163.5 3.4 pad_maximum_fusion
  166.9 0.0 reduce-scatter.2.cloned.1.call-update
  167.0 0.2 all-reduce.4.cloned.1.call-start
  167.2 2.8 copy.21
  170.0 3.2 pad_slice_fusion
  173.2 4.9 %copy.20 = bf16[7,128,1536]{2,1,0:T(8,128)(2,1)} copy(bf16[7,128,1536]{1,2,0:T(8,128)(2,1)} %get-tuple-element.7) | data formatting | bytes 5505024 | tf_op jit(solution)/shard_map/slice | solution.py:70
  178.1 0.0 copy-done.3
  178.1 2.8 copy.22
  180.9 2.7 all-gather.2.cloned.1.call-done
  183.7 6.5 %fusion.15 = f32[896,768]{1,0:T(8,128)} fusion(bf16[896,1536]{1,0:T(8,128)(2,1)} %bitcast.47, bf16[1536,3,768]{2,0,1:T(8,128)(2,1)} %all-gather.2.cloned.1.call-done), kind=kOutput, calls=%fused_computation.32 | convolution fusion | flops 2113929216 | bytes 7864320 | tf_op jit(solution)/shard_map/dot_general | solution.py:79
  190.2 130.5 %reduce-scatter.2.cloned.1.call-done = bf16[384,3,768]{2,0,1:T(8,128)(2,1)} async-done(((bf16[1536,3,768]{2,0,1:T(8,128)(2,1)}), bf16[384,3,768]{2,0,1:T(8,128)(2,1)}) %reduce-scatter.2.cloned.1.call-update) | async-done | bytes 1769488 | tf_op jit(solution)/shard_map/reduce_scatter | solution.py:97
  320.6 0.0 all-reduce.4.cloned.1.call-update
  320.6 0.0 copy-done.5
  320.6 0.0 copy-start.6
  320.7 0.0 copy-start.11
  320.7 4.1 %fusion.14 = f32[896,768]{1,0:T(8,128)S(1)} fusion(bf16[896,1536]{1,0:T(8,128)(2,1)S(1)} %bitcast.45, bf16[1536,3,768]{2,0,1:T(8,128)(2,1)} %all-gather.2.cloned.1.call-done), kind=kOutput, calls=%fused_computation.30 | convolution fusion | flops 2113929216 | bytes 7864320 | tf_op jit(solution)/shard_map/dot_general | solution.py:79
  324.8 0.0 copy-done.6
  324.8 0.0 copy-done.11
  324.8 5.5 %add_add_fusion = f32[896,768]{1,0:T(8,128)} fusion(f32[896,768]{1,0:T(8,128)S(1)} %copy-done.11, f32[896,768]{1,0:T(8,128)S(1)} %fusion.14, bf16[896,1536]{1,0:T(8,128)(2,1)S(1)} %bitcast.46, bf16[1536,3,768]{2,0,1:T(8,128)(2,1)} %all-gather.2.cloned.1.call-done), kind=kOutput, calls=%fused_computation.26 | convolution fusion | flops 2115305472 | bytes 13369344 | tf_op jit(solution)/shard_map/dot_general | solution.py:79
  330.3 3.6 %copy.23 = f32[7,128,768]{1,2,0:T(8,128)} copy(f32[7,128,768]{2,1,0:T(8,128)} %bitcast.48) | data formatting | bytes 5505024 | tf_op jit(solution)/shard_map/reshape | solution.py:83
  333.9 0.0 copy-done.2
  333.9 3.2 fusion.9
  337.1 2.5 copy.29
  339.6 4.7 %all-reduce.4.cloned.1.call-done = bf16[384,3,768]{2,0,1:T(8,128)(2,1)} async-done(((bf16[384,3,768]{2,0,1:T(8,128)(2,1)}), bf16[384,3,768]{2,0,1:T(8,128)(2,1)}) %all-reduce.4.cloned.1.call-update) | async-done | bytes 1769488 | tf_op jit(solution)/shard_map/psum | solution.py:100
  344.3 3.6 %convert_element_type.38 = f32[384,3,768]{2,0,1:T(8,128)} convert(bf16[384,3,768]{2,0,1:T(8,128)(2,1)} %all-reduce.4.cloned.1.call-done) | non-fusion elementwise | flops 884736 | bytes 5308416 | tf_op jit(solution)/shard_map/convert_element_type | solution.py:100
  (5 shorter events, 0.0 us)
Async XLA Ops:
  7.2 176.5 %all-gather.2.cloned.1.call-start = ((), (), s32[]{:S(2)}) async-start(), calls=%async_computation.1 | async-start | bytes 8847360 | tf_op jit(solution)/shard_map/all_gather | solution.py:76
  7.9 312.7 %reduce-scatter.2.cloned.1.call-start = ((), (), s32[]{:S(2)}) async-start(), calls=%async_computation.2 | async-start | bytes 8847360 | tf_op jit(solution)/shard_map/reduce_scatter | solution.py:97
  8.6 7.8 %copy-start.9 = (s32[12]{0:T(128)S(1)}, s32[12]{0:T(128)}, u32[]{:S(2)}) copy-start(s32[12]{0:T(128)} %param.11) | copy-start | bytes 148
  12.8 9.8 %copy-start.10 = (pred[12]{0:T(512)(128)(4,1)S(1)}, pred[12]{0:T(512)(128)(4,1)}, u32[]{:S(2)}) copy-start(pred[12]{0:T(512)(128)(4,1)} %constant.29.clone.1) | copy-start | bytes 40
  12.8 50.4 %collective-permute-start = (bf16[6,128,768]{1,2,0:T(8,128)(2,1)}, bf16[6,128,768]{1,2,0:T(8,128)(2,1)S(1)}, u32[]{:S(2)}, u32[]{:S(2)}) collective-permute-start(bf16[6,128,768]{1,2,0:T(8,128)(2,1)} %constant_dynamic-slice_fusion.1), channel_id=1, source_target_pairs={{0,4},{4,8},{8,12},{12,0},{1,5},{5,9},{9,13},{13,1},{2,6},{6,10},{... | collective-permute-start | bytes 3538952 | tf_op jit(solution)/shard_map/ppermute | solution.py:12
  16.5 46.4 %collective-permute-start.1 = (bf16[6]{0:T(256)(128)(2,1)S(1)}, bf16[6]{0:T(256)(128)(2,1)S(1)}, u32[]{:S(2)}, u32[]{:S(2)}) collective-permute-start(bf16[6]{0:T(256)(128)(2,1)S(1)} %get-tuple-element.12), channel_id=1, source_target_pairs={{0,4},{4,8},{8,12},{12,0},{1,5},{5,9},{9,13},{13,1},{2,6},{6,10},{... | collective-permute-start | bytes 44 | tf_op jit(solution)/shard_map/ppermute | solution.py:12
  22.6 40.7 %copy-start.8 = (f32[768]{0:T(1024)S(1)}, f32[768]{0:T(1024)}, u32[]{:S(2)}) copy-start(f32[768]{0:T(1024)} %param.9) | copy-start | bytes 9220
  26.3 48.8 %copy-start = (bf16[12,128,768]{1,2,0:T(8,128)(2,1)S(1)}, bf16[12,128,768]{1,2,0:T(8,128)(2,1)}, u32[]{:S(2)}) copy-start(bf16[12,128,768]{1,2,0:T(8,128)(2,1)} %copy.24) | copy-start | bytes 7077892
  63.3 13.0 %copy-start.1 = (bf16[12,128,768]{1,2,0:T(8,128)(2,1)}, bf16[12,128,768]{1,2,0:T(8,128)(2,1)S(1)}, u32[]{:S(2)}) copy-start(bf16[12,128,768]{1,2,0:T(8,128)(2,1)S(1)} %constant_dynamic-update-slice_fusion.1) | copy-start | bytes 7077892
  73.4 76.1 %copy-start.4 = (bf16[7,128,768]{1,2,0:T(8,128)(2,1)}, bf16[7,128,768]{1,2,0:T(8,128)(2,1)S(1)}, u32[]{:S(2)}) copy-start(bf16[7,128,768]{1,2,0:T(8,128)(2,1)S(1)} %fusion.7) | copy-start | bytes 4128772
  73.4 76.1 %collective-permute-start.2 = (bf16[7,128,768]{1,2,0:T(8,128)(2,1)S(1)}, bf16[7,128,768]{1,2,0:T(8,128)(2,1)}, u32[]{:S(2)}, u32[]{:S(2)}) collective-permute-start(bf16[7,128,768]{1,2,0:T(8,128)(2,1)S(1)} %fusion.7), channel_id=1, source_target_pairs={{0,2},{2,0},{1,3},{3,1},{4,6},{6,4},{5,7},{7,5},{8,10},{10,8},{9,1... | collective-permute-start | bytes 4128776 | tf_op jit(solution)/shard_map/ppermute | solution.py:58
  76.3 72.1 %collective-permute-start.3 = (bf16[6,128,768]{1,2,0:T(8,128)(2,1)}, bf16[6,128,768]{1,2,0:T(8,128)(2,1)S(1)}, u32[]{:S(2)}, u32[]{:S(2)}) collective-permute-start(bf16[6,128,768]{1,2,0:T(8,128)(2,1)} %constant_dynamic-slice_fusion), channel_id=1, source_target_pairs={{0,4},{4,8},{8,12},{12,0},{1,5},{5,9},{9,13},{13,1},{2,6},{6,10},{... | collective-permute-start | bytes 3538952 | tf_op jit(solution)/shard_map/ppermute | solution.py:12
  149.5 5.2 %copy-start.7 = (bf16[12,128,768]{1,2,0:T(8,128)(2,1)S(1)}, bf16[12,128,768]{1,2,0:T(8,128)(2,1)}, u32[]{:S(2)}) copy-start(bf16[12,128,768]{1,2,0:T(8,128)(2,1)} %constant_dynamic-update-slice_fusion) | copy-start | bytes 7077892
  167.0 177.3 %all-reduce.4.cloned.1.call-start = ((), (), s32[]{:S(2)}) async-start(), calls=%async_computation.3 | async-start | bytes 3538944 | tf_op jit(solution)/shard_map/psum | solution.py:100
  173.2 4.9 %copy-start.3 = (bf16[7,128,1536]{1,2,0:T(8,128)(2,1)S(1)}, bf16[7,128,1536]{1,2,0:T(8,128)(2,1)}, u32[]{:S(2)}) copy-start(bf16[7,128,1536]{1,2,0:T(8,128)(2,1)} %get-tuple-element.6) | copy-start | bytes 8257540
  183.7 137.0 %copy-start.5 = (bf16[7,128,1536]{2,1,0:T(8,128)(2,1)S(1)}, bf16[7,128,1536]{2,1,0:T(8,128)(2,1)}, u32[]{:S(2)}) copy-start(bf16[7,128,1536]{2,1,0:T(8,128)(2,1)} %copy.21) | copy-start | bytes 8257540
  320.6 4.1 %copy-start.6 = (bf16[7,128,1536]{2,1,0:T(8,128)(2,1)S(1)}, bf16[7,128,1536]{2,1,0:T(8,128)(2,1)}, u32[]{:S(2)}) copy-start(bf16[7,128,1536]{2,1,0:T(8,128)(2,1)} %copy.22) | copy-start | bytes 8257540
  320.7 4.1 %copy-start.11 = (f32[896,768]{1,0:T(8,128)S(1)}, f32[896,768]{1,0:T(8,128)}, u32[]{:S(2)}) copy-start(f32[896,768]{1,0:T(8,128)} %fusion.15) | copy-start | bytes 8257540
  330.3 3.6 %copy-start.2 = (bf16[12,128,768]{1,2,0:T(8,128)(2,1)S(1)}, bf16[12,128,768]{1,2,0:T(8,128)(2,1)}, u32[]{:S(2)}) copy-start(bf16[12,128,768]{1,2,0:T(8,128)(2,1)} %copy-done.1) | copy-start | bytes 7077892
Sparse Core Ops, SparseCore 0:
  9.6 174.0 all-gather.1
  186.0 134.5 reduce-scatter.1
  323.0 21.2 all-reduce.3
